TPU v7x, 32 devices: a whole 2x2x4 slice. The times are simulated.
32 devices in a mesh: seq: 16 (over z, y, x), tp: 2 (over core).
Axes of the slice: x: 2, y: 2, z: 4, core: 2. Of those that a mesh axis runs over, the one named last changes fastest.
Arguments:
- latent: bfloat16 [4096, 5120], P('seq', 'tp'), may hold values from -12 to 12
- pose_rows: bfloat16 [4096, 256], P('seq'), may hold values from -6 to 6
- dest_device: int32 [4096, 1], P('seq'), may hold values from 0 to 15; in each aligned block of 256 rows (0 to 255, 256 to 511, ...) at most 32 rows name the same one
- dest_slot: int32 [4096], P('seq'), may hold values from 0 to 255
- w_section1: bfloat16 [16, 32], replicated, may hold values from -1.5 to 1.5
- w_section2: bfloat16 [128, 128], replicated, may hold values from -0.5 to 0.5
- w_section3: bfloat16 [512, 5120], P(None, 'tp'), may hold values from -0.25 to 0.25
- shift_mod: float32 [5120], P('tp'), may hold values from -3 to 3
- scale_mod: float32 [5120], P('tp'), may hold values from -0.5 to 0.5
- w_query: bfloat16 [5120, 5120], P('seq', 'tp'), may hold values from -0.078125 to 0.078125
- bias_query: float32 [5120], P('tp'), may hold values from -3 to 3
- gain_query: float32 [5120], P('tp'), may hold values from 0.25 to 1.75
- cotangent: bfloat16 [4096, 5120], P('seq', 'tp'), may hold values from -16 to 16
Outputs:
- normed_query: bfloat16 [4096, 5120], P('seq', 'tp')
- section_three_grad: float32 [512, 5120], P('seq', 'tp')
- section_two_grad: float32 [128, 128], replicated
- section_one_grad: float32 [16, 32], replicated
Inputs may be any that keep to these rules, and one draw needn't show every extreme that they name: `dest_device`: among the rows of one device no index of seq appears more than 32 times, and some index appears exactly 32 times among some device's rows.
All inputs are finite; a program needn't handle non-finite values.
Results may differ from a plain program's by a relative error of at most 0.02.
Values may be sent and summed in bfloat16 or wider, within the bound.
A program may use at most 128 MiB of HBM per device.

v0:
```python
import jax
import jax.numpy as jnp
from jax import lax
from jax.sharding import PartitionSpec as P

epsilon = 1e-06


def silu_slope(z):
    s = jax.nn.sigmoid(z)
    return s * (1.0 + z * (1.0 - s))


def run_sections(pose, w_one, w_two):
    count = pose.shape[0]
    c_one = w_one.shape[1]
    cells = pose.reshape(count * 16, 16)
    z_one = jnp.dot(cells, w_one, preferred_element_type=jnp.float32)
    feature_one = jax.nn.silu(z_one).astype(jnp.bfloat16)
    stacked_one = (
        feature_one.reshape(count, 2, 2, 2, 2, c_one)
        .transpose(0, 1, 3, 2, 4, 5)
        .reshape(count * 4, 4 * c_one)
    )
    z_two = jnp.dot(stacked_one, w_two, preferred_element_type=jnp.float32)
    stacked_two = jax.nn.silu(z_two).astype(jnp.bfloat16).reshape(count, 4 * w_two.shape[1])
    return (cells, z_one, stacked_one, z_two, stacked_two)


def section_back(cells, z_one, stacked_one, z_two, stacked_grad, w_two):
    quads = z_two.shape[0]
    count = quads // 4
    c_one = z_one.shape[1]
    two_grad = stacked_grad.reshape(quads, -1) * silu_slope(z_two)
    grad_two = lax.dot_general(
        stacked_one.astype(jnp.float32),
        two_grad,
        (((0,), (0,)), ((), ())),
        precision=lax.Precision.HIGHEST,
    )
    back_one = jnp.dot(two_grad, w_two.astype(jnp.float32).T, precision=lax.Precision.HIGHEST)
    back_one = (
        back_one.reshape(count, 2, 2, 2, 2, c_one)
        .transpose(0, 1, 3, 2, 4, 5)
        .reshape(count * 16, c_one)
    )
    one_grad = back_one * silu_slope(z_one)
    grad_one = lax.dot_general(
        cells.astype(jnp.float32),
        one_grad,
        (((0,), (0,)), ((), ())),
        precision=lax.Precision.HIGHEST,
    )
    return (grad_two, grad_one)


def body(
    latent,
    pose_rows,
    dest_device,
    dest_slot,
    w_section1,
    w_section2,
    w_section3,
    shift_mod,
    scale_mod,
    w_query,
    bias_query,
    gain_query,
    cotangent,
):
    tokens = latent.shape[0]
    seq_count = lax.axis_size("seq")
    tp_count = lax.axis_size("tp")
    full_width = latent.shape[1] * tp_count
    query_width = w_query.shape[1] * tp_count
    capacity = max(2, 2 * tokens // seq_count)
    slots_all = seq_count * capacity
    owner = dest_device[:, 0]
    marks = (owner[:, None] == jnp.arange(seq_count, dtype=jnp.int32)[None, :]).astype(jnp.int32)
    before = jnp.cumsum(marks, axis=0) - marks
    position = owner * capacity + jnp.sum(before * marks, axis=1)
    slot_send = (
        jnp.full((slots_all,), tokens, jnp.int32)
        .at[position]
        .set(dest_slot)
        .reshape(seq_count, capacity)
    )
    cells, z_one, stacked_one, z_two, stacked_two = run_sections(pose_rows, w_section1, w_section2)
    pose_tokens = jnp.dot(stacked_two, w_section3, preferred_element_type=jnp.float32).astype(
        jnp.bfloat16
    )
    outgoing = (
        jnp.zeros((slots_all, pose_tokens.shape[1]), jnp.bfloat16).at[position].set(pose_tokens)
    )
    incoming, slot_recv = (
        lax.all_to_all(
            outgoing.reshape(seq_count, capacity, -1),
            "seq",
            split_axis=0,
            concat_axis=0,
            tiled=True,
        ),
        lax.all_to_all(slot_send, "seq", split_axis=0, concat_axis=0, tiled=True),
    )
    incoming = incoming.reshape(slots_all, -1)
    select = (
        jnp.arange(tokens, dtype=jnp.int32)[:, None] == slot_recv.reshape(-1)[None, :]
    ).astype(jnp.bfloat16)
    guidance = jnp.dot(select, incoming, preferred_element_type=jnp.float32)
    summed = latent.astype(jnp.float32) + guidance
    total, squares = lax.psum((jnp.sum(summed, axis=1), jnp.sum(summed * summed, axis=1)), "tp")
    center = total / full_width
    inverse = lax.rsqrt(squares / full_width - center * center + epsilon)[:, None]
    normed = (summed - center[:, None]) * inverse
    modulated = (normed * (1.0 + scale_mod) + shift_mod).astype(jnp.bfloat16)
    whole = lax.all_gather(modulated, "tp", axis=1, tiled=True)
    weights_all = lax.all_gather(w_query, "seq", axis=0, tiled=True)
    query = jnp.dot(whole, weights_all, preferred_element_type=jnp.float32)
    query = query + bias_query
    upstream = cotangent.astype(jnp.float32) * gain_query
    sum_square, sum_along = lax.psum(
        (jnp.sum(query * query, axis=1), jnp.sum(upstream * query, axis=1)), "tp"
    )
    rinv = lax.rsqrt(sum_square / query_width + epsilon)[:, None]
    normed_query = (query * rinv * gain_query).astype(jnp.bfloat16)
    along = (sum_along / query_width)[:, None]
    query_grad = (upstream * rinv - query * along * rinv**3).astype(jnp.bfloat16)
    partial_grad = lax.dot_general(
        query_grad, weights_all, (((1,), (1,)), ((), ())), preferred_element_type=jnp.float32
    )
    modulated_grad = lax.psum_scatter(
        partial_grad.astype(jnp.bfloat16), "tp", scatter_dimension=1, tiled=True
    ).astype(jnp.float32)
    normed_grad = modulated_grad * (1.0 + scale_mod)
    grad_total, grad_cross = lax.psum(
        (jnp.sum(normed_grad, axis=1), jnp.sum(normed_grad * normed, axis=1)), "tp"
    )
    latent_grad = inverse * (
        normed_grad
        - (grad_total / full_width)[:, None]
        - normed * (grad_cross / full_width)[:, None]
    )
    latent_grad = latent_grad.astype(jnp.bfloat16)
    slot_grad = lax.dot_general(
        select, latent_grad, (((0,), (0,)), ((), ())), preferred_element_type=jnp.float32
    ).astype(jnp.bfloat16)
    returned = lax.all_to_all(
        slot_grad.reshape(seq_count, capacity, -1), "seq", split_axis=0, concat_axis=0, tiled=True
    )
    row_grad = returned.reshape(slots_all, -1)[position]
    section_three_grad = lax.psum_scatter(
        lax.dot_general(
            stacked_two, row_grad, (((0,), (0,)), ((), ())), preferred_element_type=jnp.float32
        ),
        "seq",
        scatter_dimension=0,
        tiled=True,
    )
    stacked_grad = lax.dot_general(
        row_grad, w_section3, (((1,), (1,)), ((), ())), preferred_element_type=jnp.float32
    )
    grad_two, grad_one = section_back(cells, z_one, stacked_one, z_two, stacked_grad, w_section2)
    section_two_grad, section_one_grad = lax.psum((grad_two, grad_one), ("seq", "tp"))
    return (normed_query, section_three_grad, section_two_grad, section_one_grad)


def solution(mesh):
    return jax.shard_map(
        body,
        mesh=mesh,
        in_specs=(
            P("seq", "tp"),
            P("seq", None),
            P("seq", None),
            P("seq"),
            P(),
            P(),
            P(None, "tp"),
            P("tp"),
            P("tp"),
            P("seq", "tp"),
            P("tp"),
            P("tp"),
            P("seq", "tp"),
        ),
        out_specs=(P("seq", "tp"), P("seq", "tp"), P(), P()),
        check_vma=False,
    )
```

profile of v0, /device:TPU:0, one launch (start us, length us, event | category | flops | bytes accessed | tf_op | source)
XLA Modules:
  0.0 788.0 jit_solution(6499666152220375031)
XLA Ops:
  7.2 0.0 copy-start
  7.2 0.8 fusion.23
  8.0 0.6 reduce-window.6
  8.6 0.2 slice_reduce_fusion
  8.8 0.8 fusion.22
  9.6 0.7 compare_select_fusion
  10.3 1.6 scatter_custom_fusion
  11.8 0.7 all_to_all.12
  12.5 8.3 %all-to-all-start = ((s32[16,1,32]{2,1,0:T(1,128)}), s32[16,1,32]{2,1,0:T(1,128)S(1)}, u32[]{:S(2)}, u32[]{:S(2)}) async-start(s32[16,1,32]{2,1,0:T(1,128)} %all_to_all.12), calls=%async_computation | async-start | bytes 16384 | tf_op jit(solution)/shard_map/all_to_all | solution.py:104
  20.8 2.6 reshape.78
  23.4 2.5 multiply_convert_fusion.4
  25.9 1.3 copy.19
  27.3 2.9 copy.20
  30.2 2.9 reshape.80
  33.1 0.0 copy-start.1
  33.1 1.0 multiply_convert_fusion.3
  34.1 0.2 reshape.81
  34.3 1.9 convolution_convert_fusion.2
  36.2 5.1 scatter_custom_fusion.1
  41.3 7.1 all-to-all-start.1
  48.4 0.0 all-gather.3.cloned.1.call-start
  48.5 0.5 broadcast.89
  49.0 0.7 reduce.5
  49.7 0.1 eq.49
  49.8 50.4 %all-to-all-done.1 = bf16[16,32,2560]{2,1,0:T(8,128)(2,1)} async-done(((bf16[16,32,2560]{2,1,0:T(8,128)(2,1)}), bf16[16,32,2560]{2,1,0:T(8,128)(2,1)}, u32[]{:S(2)}, u32[]{:S(2)}) %all-to-all-start.1) | async-done | bytes 2621472 | tf_op jit(solution)/shard_map/all_to_all | solution.py:97
  100.2 4.6 fusion.27
  104.8 2.4 all-reduce.2
  107.3 3.4 add_convert_fusion
  110.7 0.0 all-gather.3.cloned.1.call-update
  110.7 0.0 all-gather.5.cloned.1.call-start
  110.7 0.7 all-gather.5.cloned.1.call-update
  111.4 0.2 reduce-scatter.3.cloned.1.call-start
  111.7 16.9 %all-gather.3.cloned.1.call-done = bf16[256,5120]{1,0:T(8,128)(2,1)} async-done(((bf16[256,2560]{1,0:T(8,128)(2,1)}), bf16[256,5120]{1,0:T(8,128)(2,1)}) %all-gather.3.cloned.1.call-update) | async-done | bytes 2621456 | tf_op jit(solution)/shard_map/all_gather | solution.py:117
  128.5 285.4 %all-gather.5.cloned.1.call-done = bf16[5120,2560]{1,0:T(8,128)(2,1)} async-done(((bf16[320,2560]{1,0:T(8,128)(2,1)}), bf16[5120,2560]{1,0:T(8,128)(2,1)}) %all-gather.5.cloned.1.call-update) | async-done | bytes 26214416 | tf_op jit(solution)/shard_map/all_gather | solution.py:118
  413.9 14.3 %multiply_reduce_fusion.1 = (f32[256]{0:T(256)S(1)}, f32[256]{0:T(256)S(1)}, f32[256,2560]{1,0:T(8,128)}) fusion(bf16[256,2560]{1,0:T(8,128)(2,1)} %param.25, f32[2560]{0:T(1024)S(1)} %copy-done.4, f32[2560]{0:T(1024)S(1)} %copy-done.6, bf16[256,5120]{1,0:T(8,128)(2,1)} %all-gather.3.cloned.1.call-done, bf16[5120,2560]{1,0:T(8,128)(2,1)} %all-gather.5.cloned.1.call-done), kind=kOutput, calls=%fused_computation.13 | convolution fusion | flops 6715473920 | bytes 32790528 | tf_op jit(solution)/shard_map/dot_general | solution.py:119
  428.2 2.4 all-reduce.1
  430.7 14.8 %convolution_convert_fusion = bf16[256,5120]{1,0:T(8,128)(2,1)} fusion(bf16[5120,2560]{1,0:T(8,128)(2,1)} %all-gather.5.cloned.1.call-done, f32[256,2560]{1,0:T(8,128)} %get-tuple-element.25, bf16[256,2560]{1,0:T(8,128)(2,1)} %param.25, f32[256]{0:T(256)S(1)} %get-tuple-element.16, f32[256]{0:T(256)S(1)} %get-tuple-element.26, f32[2560]{0:T(1024)S(1)} %copy-done.4, ...), kind=kOutput, calls=%fused_computation.3 | convolution fusion | flops 6716784640 | bytes 32781312 | tf_op jit(solution)/shard_map/dot_general | solution.py:129
  445.5 0.0 reduce-scatter.3.cloned.1.call-update
  445.5 8.5 %reduce-scatter.3.cloned.1.call-done = bf16[256,2560]{1,0:T(8,128)(2,1)} async-done(((bf16[256,5120]{1,0:T(8,128)(2,1)}), bf16[256,2560]{1,0:T(8,128)(2,1)}) %reduce-scatter.3.cloned.1.call-update) | async-done | bytes 1310736 | tf_op jit(solution)/shard_map/reduce_scatter | solution.py:132
  454.1 2.9 fusion
  456.9 2.5 all-reduce
  459.4 4.9 convolution_convert_fusion.1
  464.3 6.9 all-to-all-start.2
  471.2 0.3 all-reduce.5.cloned.1.call-start
  471.5 51.9 %all-to-all-done.2 = bf16[16,32,2560]{2,1,0:T(8,128)(2,1)} async-done(((bf16[16,32,2560]{2,1,0:T(8,128)(2,1)}), bf16[16,32,2560]{2,1,0:T(8,128)(2,1)}, u32[]{:S(2)}, u32[]{:S(2)}) %all-to-all-start.2) | async-done | bytes 2621472 | tf_op jit(solution)/shard_map/all_to_all | solution.py:148
  523.4 5.9 gather_fusion
  529.2 2.2 fusion.29
  531.4 0.8 reshape.86
  532.3 1.4 multiply_multiply_fusion
  533.6 2.0 fusion.30
  535.7 0.0 all-reduce.5.cloned.1.call-update
  535.7 0.0 reduce-scatter.5.cloned.1.call-start
  535.7 4.5 fusion.28
  540.2 0.0 reduce-scatter.5.cloned.1.call-update
  540.3 3.1 multiply_convert_fusion.1
  543.3 1.2 fusion.31
  544.5 3.9 reshape.87
  548.4 3.7 copy.21
  552.1 2.2 copy.22
  554.3 2.4 convolution_bitcast_fusion
  556.7 48.4 %psum.63 = f32[16,32]{1,0:T(8,128)} all-reduce(f32[16,32]{1,0:T(8,128)S(1)} %convolution_bitcast_fusion), channel_id=1, replica_groups=mesh['seq'=16,'tp'=2] {'seq','tp'}, use_global_device_ids=true, to_apply=%region_20.21 | all-reduce | flops 512 | bytes 4096 | tf_op jit(solution)/shard_map/psum | solution.py:164
  605.1 55.8 %all-reduce.5.cloned.1.call-done = f32[128,128]{1,0:T(8,128)} async-done(((f32[128,128]{1,0:T(8,128)}), f32[128,128]{1,0:T(8,128)}) %all-reduce.5.cloned.1.call-update) | async-done | bytes 65552 | tf_op jit(solution)/shard_map/psum | solution.py:164
  660.9 119.2 %reduce-scatter.5.cloned.1.call-done = f32[32,2560]{1,0:T(8,128)} async-done(((f32[512,2560]{1,0:T(8,128)}), f32[32,2560]{1,0:T(8,128)}) %reduce-scatter.5.cloned.1.call-update) | async-done | bytes 327696 | tf_op jit(solution)/shard_map/reduce_scatter | solution.py:152
  780.0 1.5 copy.26
  (21 shorter events, 0.1 us)
Async XLA Ops:
  7.2 27.1 %copy-start = (bf16[512,2560]{1,0:T(8,128)(2,1)S(1)}, bf16[512,2560]{1,0:T(8,128)(2,1)}, u32[]{:S(2)}) copy-start(bf16[512,2560]{1,0:T(8,128)(2,1)} %param.19) | copy-start | bytes 7864324
  12.5 28.8 %all-to-all-start = ((s32[16,1,32]{2,1,0:T(1,128)}), s32[16,1,32]{2,1,0:T(1,128)S(1)}, u32[]{:S(2)}, u32[]{:S(2)}) async-start(s32[16,1,32]{2,1,0:T(1,128)} %all_to_all.12), calls=%async_computation | async-start | bytes 16384 | tf_op jit(solution)/shard_map/all_to_all | solution.py:104
  25.9 7.1 copy-start.2
  33.1 3.1 copy-start.1
  41.3 7.1 copy-start.5
  41.3 58.9 %all-to-all-start.1 = ((bf16[16,32,2560]{2,1,0:T(8,128)(2,1)}), bf16[16,32,2560]{2,1,0:T(8,128)(2,1)}, u32[]{:S(2)}, u32[]{:S(2)}) async-start(bf16[16,32,2560]{2,1,0:T(8,128)(2,1)} %bitcast.53), calls=%async_computation.1 | async-start | bytes 5242880 | tf_op jit(solution)/shard_map/all_to_all | solution.py:97
  48.4 80.1 %all-gather.3.cloned.1.call-start = ((), (), s32[]{:S(2)}) async-start(), calls=%async_computation.5 | async-start | bytes 3932160 | tf_op jit(solution)/shard_map/all_gather | solution.py:117
  100.2 7.1 copy-start.3
  107.3 306.6 %copy-start.4 = (f32[2560]{0:T(1024)S(1)}, f32[2560]{0:T(1024)}, u32[]{:S(2)}) copy-start(f32[2560]{0:T(1024)} %param.24) | copy-start | bytes 30724
  107.3 306.6 %copy-start.6 = (f32[2560]{0:T(1024)S(1)}, f32[2560]{0:T(1024)}, u32[]{:S(2)}) copy-start(f32[2560]{0:T(1024)} %param.23) | copy-start | bytes 30724
  110.7 303.2 %all-gather.5.cloned.1.call-start = ((), (), s32[]{:S(2)}) async-start(), calls=%async_computation.6 | async-start | bytes 27852800 | tf_op jit(solution)/shard_map/all_gather | solution.py:118
  111.4 342.6 %reduce-scatter.3.cloned.1.call-start = ((), (), s32[]{:S(2)}) async-start(), calls=%async_computation.7 | async-start | bytes 3932160 | tf_op jit(solution)/shard_map/reduce_scatter | solution.py:132
  464.3 59.0 %all-to-all-start.2 = ((bf16[16,32,2560]{2,1,0:T(8,128)(2,1)}), bf16[16,32,2560]{2,1,0:T(8,128)(2,1)}, u32[]{:S(2)}, u32[]{:S(2)}) async-start(bf16[16,32,2560]{2,1,0:T(8,128)(2,1)} %bitcast.57), calls=%async_computation.3 | async-start | bytes 5242880 | tf_op jit(solution)/shard_map/all_to_all | solution.py:148
  471.2 189.7 %all-reduce.5.cloned.1.call-start = ((), (), s32[]{:S(2)}) async-start(), calls=%async_computation.9 | async-start | bytes 131072 | tf_op jit(solution)/shard_map/psum | solution.py:164
  535.7 244.3 %reduce-scatter.5.cloned.1.call-start = ((), (), s32[]{:S(2)}) async-start(), calls=%async_computation.8 | async-start | bytes 5570560 | tf_op jit(solution)/shard_map/reduce_scatter | solution.py:152
Sparse Core Ops, SparseCore 0:
  110.8 17.6 all-gather.2
  131.2 282.6 all-gather.4
  445.6 8.3 reduce-scatter.2
  535.8 125.0 all-reduce.4
  663.7 116.2 reduce-scatter.4
where the time goes:
time: 789 us; the launch traced here: 788 us
  waiting for transfers between devices  589 us (75%)
  matrix products  56.4 us (7%)
  blocking collectives  55.7 us (7%)
  local copies, waits for them, and re-layouts  36 us (5%)
  starting transfers between devices  22.9 us (3%)
  other arithmetic  14.3 us (2%)
  between operations  13.9 us (2%)
    all_gather x1, waiting for transfers between devices, body(): weights_all = lax.all_gather(w_query, 'seq', axis=0, tiled=True)  285 us
    reduce_scatter x1, waiting for transfers between devices, body(): lax.psum_scatter(lax.dot_general(stacked_two, row_grad, (((0,), (0,)), ((...  119 us
    psum x1, waiting for transfers between devices, body(): lax.psum((grad_two, grad_one), ('seq', 'tp'))  55.8 us
    all_to_all x1, waiting for transfers between devices, body(): lax.all_to_all(slot_grad.reshape(seq_count, capacity, -1), 'seq', split_a...  51.9 us
    all_to_all x1, waiting for transfers between devices, body(): lax.all_to_all(outgoing.reshape(seq_count, capacity, -1), 'seq', split_ax...  50.4 us
    psum x1, blocking collectives, body(): lax.psum((grad_two, grad_one), ('seq', 'tp'))  48.4 us
    all_gather x1, waiting for transfers between devices, body(): whole = lax.all_gather(modulated, 'tp', axis=1, tiled=True)  16.9 us
  transfers between devices with their start and end apart: 8, of which 7 were waited for; matrix products, arithmetic and copies ran while one was open for 5% of the time, Pallas kernels for 0%

commit v1 on v0

v1 whole, which is shorter than its diff:
```python
import jax
import jax.numpy as jnp
import numpy as np
from jax import lax
from jax.sharding import PartitionSpec as P

epsilon = 1e-06
F32, BF16 = jnp.float32, jnp.bfloat16


def silu_slope(z):
    s = jax.nn.sigmoid(z)
    return s * (1.0 + z * (1.0 - s))


def mm(a, b):
    return jnp.dot(a, b, preferred_element_type=F32)


def mm_nt(a, b):
    return lax.dot_general(a, b, (((1,), (1,)), ((), ())), preferred_element_type=F32)


def mm_tn(a, b):
    return lax.dot_general(a, b, (((0,), (0,)), ((), ())), preferred_element_type=F32)


def cell_places():
    table = np.zeros((16, 16), np.float32)
    for i in range(4):
        for j in range(4):
            place = ((i // 2) * 2 + j // 2) * 4 + (i % 2) * 2 + j % 2
            table[4 * i + j, place] = 1.0
    return jnp.asarray(table)


def spread_one(w_one):
    depth, c_one = w_one.shape
    wide = cell_places()[:, None, :, None] * w_one.astype(F32)[None, :, None, :]
    return wide.reshape(16 * depth, 16 * c_one).astype(BF16)


def fold_one(wide, depth, c_one):
    blocks = wide.reshape(16, depth, 16, c_one) * cell_places()[:, None, :, None]
    return jnp.sum(blocks, axis=(0, 2))


def dispatch(pose_rows, dest_device, dest_slot, seq_count):
    count, width = pose_rows.shape
    capacity = max(2, 2 * count // seq_count)
    slots_all = seq_count * capacity
    owner = dest_device[:, 0]
    marks = (owner[:, None] == jnp.arange(seq_count, dtype=jnp.int32)[None, :]).astype(BF16)
    index = jnp.arange(count, dtype=jnp.int32)
    lower = (index[:, None] > index[None, :]).astype(BF16)
    before = mm(lower, marks)
    rank = jnp.sum(before * marks.astype(F32), axis=1).astype(jnp.int32)
    position = owner * capacity + rank
    place = (jnp.arange(slots_all, dtype=jnp.int32)[:, None] == position[None, :]).astype(BF16)
    lane = jnp.arange(128, dtype=jnp.int32)[None, :]
    slot = dest_slot[:, None]
    tail = jnp.where(lane == 0, slot // 128, jnp.where(lane == 1, slot % 128, jnp.where(lane == 2, 1, 0)))
    rows = jnp.concatenate([pose_rows, tail.astype(BF16)], axis=1)
    outgoing = mm(place, rows).astype(BF16)
    incoming = lax.all_to_all(
        outgoing.reshape(seq_count, capacity, width + 128), "seq", split_axis=0, concat_axis=0, tiled=True
    ).reshape(slots_all, width + 128)
    info = incoming[:, width : width + 3].astype(F32)
    slot_recv = (info[:, 0] * 128.0 + info[:, 1]).astype(jnp.int32)
    slot_recv = jnp.where(info[:, 2] > 0.5, slot_recv, -1)
    return incoming[:, :width], slot_recv


def body(
    latent,
    pose_rows,
    dest_device,
    dest_slot,
    w_section1,
    w_section2,
    w_section3,
    shift_mod,
    scale_mod,
    w_query,
    bias_query,
    gain_query,
    cotangent,
):
    tokens = latent.shape[0]
    seq_count = lax.axis_size("seq")
    tp_count = lax.axis_size("tp")
    full_width = latent.shape[1] * tp_count
    query_width = w_query.shape[1] * tp_count
    depth, c_one = w_section1.shape
    c_two = w_section2.shape[1]
    weights_all = lax.all_gather(w_query, "seq", axis=0, tiled=True)
    pose_in, slot_recv = dispatch(pose_rows, dest_device, dest_slot, seq_count)
    w_wide = spread_one(w_section1)
    w_quad = jnp.kron(jnp.eye(4, dtype=BF16), w_section2)
    z_one = mm(pose_in, w_wide)
    stacked_one = jax.nn.silu(z_one).astype(BF16)
    z_two = mm(stacked_one, w_quad)
    stacked_two = jax.nn.silu(z_two).astype(BF16)
    select = (jnp.arange(tokens, dtype=jnp.int32)[:, None] == slot_recv[None, :]).astype(BF16)
    token_two = mm(select, stacked_two).astype(BF16)
    guidance = mm(token_two, w_section3)
    summed = latent.astype(F32) + guidance
    total, squares = lax.psum((jnp.sum(summed, axis=1), jnp.sum(summed * summed, axis=1)), "tp")
    center = total / full_width
    inverse = lax.rsqrt(squares / full_width - center * center + epsilon)[:, None]
    normed = (summed - center[:, None]) * inverse
    modulated = (normed * (1.0 + scale_mod) + shift_mod).astype(BF16)
    whole = lax.all_gather(modulated, "tp", axis=1, tiled=True)
    query = mm(whole, weights_all) + bias_query
    upstream = cotangent.astype(F32) * gain_query
    sum_square, sum_along = lax.psum(
        (jnp.sum(query * query, axis=1), jnp.sum(upstream * query, axis=1)), "tp"
    )
    rinv = lax.rsqrt(sum_square / query_width + epsilon)[:, None]
    normed_query = (query * rinv * gain_query).astype(BF16)
    along = (sum_along / query_width)[:, None]
    query_grad = (upstream * rinv - query * along * rinv**3).astype(BF16)
    partial_grad = mm_nt(query_grad, weights_all)
    modulated_grad = lax.psum_scatter(
        partial_grad.astype(BF16), "tp", scatter_dimension=1, tiled=True
    ).astype(F32)
    normed_grad = modulated_grad * (1.0 + scale_mod)
    grad_total, grad_cross = lax.psum(
        (jnp.sum(normed_grad, axis=1), jnp.sum(normed_grad * normed, axis=1)), "tp"
    )
    latent_grad = inverse * (
        normed_grad
        - (grad_total / full_width)[:, None]
        - normed * (grad_cross / full_width)[:, None]
    )
    latent_grad = latent_grad.astype(BF16)
    section_three_grad = lax.psum_scatter(
        mm_tn(token_two, latent_grad).astype(BF16), "seq", scatter_dimension=0, tiled=True
    ).astype(F32)
    token_grad = mm_nt(latent_grad, w_section3).astype(BF16)
    stacked_grad = mm_tn(select, token_grad)
    two_grad = (stacked_grad * silu_slope(z_two)).astype(BF16)
    wide_two = mm_tn(stacked_one, two_grad)
    grad_two = sum(
        wide_two[4 * c_one * q : 4 * c_one * (q + 1), c_two * q : c_two * (q + 1)] for q in range(4)
    )
    one_grad = (mm_nt(two_grad, w_quad) * silu_slope(z_one)).astype(BF16)
    grad_one = fold_one(mm_tn(pose_in, one_grad), depth, c_one)
    packed = jnp.concatenate([grad_two.reshape(-1), grad_one.reshape(-1)])
    packed = lax.psum(packed, ("seq", "tp"))
    cut = grad_two.size
    return (
        normed_query,
        section_three_grad,
        packed[:cut].reshape(grad_two.shape),
        packed[cut:].reshape(grad_one.shape),
    )


def solution(mesh):
    return jax.shard_map(
        body,
        mesh=mesh,
        in_specs=(
            P("seq", "tp"),
            P("seq", None),
            P("seq", None),
            P("seq"),
            P(),
            P(),
            P(None, "tp"),
            P("tp"),
            P("tp"),
            P("seq", "tp"),
            P("tp"),
            P("tp"),
            P("seq", "tp"),
        ),
        out_specs=(P("seq", "tp"), P("seq", "tp"), P(), P()),
        check_vma=False,
    )
```

time: 789 us -> 618 us (0.78)
  waiting for transfers between devices: 589 us -> 506 us
  blocking collectives: 55.7 us -> 7.36 us
  local copies, waits for them, and re-layouts: 36 us -> 9.33 us
  starting transfers between devices: 22.9 us -> 8.71 us
  other arithmetic: 14.3 us -> 23.2 us
  matrix products: 56.4 us -> 48.5 us
    all_to_all x3 -> x1, waiting for transfers between devices: 102 us -> 6.67 us  [dispatch(): lax.all_to_all(outgoing.reshape(seq_count, capacity, width + 128), 'seq',...]
    psum x1, waiting for transfers between devices: 55.8 us -> 112 us  [body(): packed = lax.psum(packed, ('seq', 'tp'))]
    psum x1 -> x0, blocking collectives: 48.4 us -> none  [body(): lax.psum((grad_two, grad_one), ('seq', 'tp'))]
    reduce_scatter x2, waiting for transfers between devices: 128 us -> 92.1 us  [the longest x1 83.8 us: body(): lax.psum_scatter(mm_tn(token_two, latent_grad).astype(BF16), 'seq', scatt...]
    all_to_all x3 -> x1, starting transfers between devices: 22.3 us -> 8.32 us  [dispatch(): lax.all_to_all(outgoing.reshape(seq_count, capacity, width + 128), 'seq',...]
    reshape x6 -> x3, local copies, waits for them, and re-layouts: 12.6 us -> 2.66 us  [the longest x1 1.9 us: fold_one(): wide.reshape(16, depth, 16, c_one) * cell_places()[:, None, :, None]]
    all_gather x1, waiting for transfers between devices: 16.9 us -> 8.67 us  [body(): whole = lax.all_gather(modulated, 'tp', axis=1, tiled=True)]
    dot_general x12, matrix products: 56.4 us -> 48.5 us  [the longest x7 21.1 us: mm(): return jnp.dot(a, b, preferred_element_type=F32)]
  transfers between devices with their start and end apart: 8 -> 6, of which waited for: 7 -> 6; matrix products, arithmetic and copies ran while one was open for 5% -> 3% of each run, Pallas kernels for 0% -> 0%
where the time goes in v1:
time: 618 us; the launch traced here: 617 us
  waiting for transfers between devices  506 us (82%)
  matrix products  48.5 us (8%)
  other arithmetic  23.2 us (4%)
  between operations  14 us (2%)
  local copies, waits for them, and re-layouts  9.33 us (2%)
  starting transfers between devices  8.71 us (1%)
  blocking collectives  7.36 us (1%)
    all_gather x1, waiting for transfers between devices, body(): weights_all = lax.all_gather(w_query, 'seq', axis=0, tiled=True)  285 us
    psum x1, waiting for transfers between devices, body(): packed = lax.psum(packed, ('seq', 'tp'))  112 us
    reduce_scatter x1, waiting for transfers between devices, body(): lax.psum_scatter(mm_tn(token_two, latent_grad).astype(BF16), 'seq', scatt...  83.8 us
    dot_general x7, matrix products, mm(): return jnp.dot(a, b, preferred_element_type=F32)  21.1 us
    dot_general x1, matrix products, mm_nt(): lax.dot_general(a, b, (((1,), (1,)), ((), ())), preferred_element_type=F32)  14.8 us
    dot_general x4, matrix products, mm_tn(): lax.dot_general(a, b, (((0,), (0,)), ((), ())), preferred_element_type=F32)  12.6 us
  transfers between devices with their start and end apart: 6, of which 6 were waited for; matrix products, arithmetic and copies ran while one was open for 3% of the time, Pallas kernels for 0%

profile of v1, /device:TPU:0, one launch (start us, length us, event | category | flops | bytes accessed | tf_op | source)
XLA Modules:
  0.0 617.0 jit_solution(16197317833480250135)
XLA Ops:
  7.2 0.0 copy-start
  7.2 0.0 copy-start.9
  7.2 0.0 copy-start.6
  7.2 1.0 fusion.8
  8.3 0.7 convert_add_fusion
  9.0 0.7 and_select_fusion.1
  9.6 0.1 select_convert_fusion
  9.8 2.0 convolution_convert_fusion.2
  11.7 8.3 %all-to-all-start = ((bf16[16,32,384]{2,1,0:T(8,128)(2,1)}), bf16[16,32,384]{2,1,0:T(8,128)(2,1)S(1)}, u32[]{:S(2)}, u32[]{:S(2)}) async-start(bf16[16,32,384]{2,1,0:T(8,128)(2,1)} %bitcast.34), calls=%async_computation | async-start | bytes 786432 | tf_op jit(solution)/shard_map/all_to_all | solution.py:65
  20.1 0.0 all-gather.3.cloned.1.call-start
  20.1 0.7 convert_element_type.105
  20.8 1.9 multiply_convert_fusion.2
  22.7 2.2 convert_element_type.107
  24.9 0.0 copy-done.9
  25.0 0.0 copy-done.6
  25.0 1.1 broadcast_multiply_fusion
  26.0 6.7 %all-to-all-done = bf16[16,32,384]{2,1,0:T(8,128)(2,1)S(1)} async-done(((bf16[16,32,384]{2,1,0:T(8,128)(2,1)}), bf16[16,32,384]{2,1,0:T(8,128)(2,1)S(1)}, u32[]{:S(2)}, u32[]{:S(2)}) %all-to-all-start) | async-done | bytes 393248 | tf_op jit(solution)/shard_map/all_to_all | solution.py:65
  32.7 0.3 fusion.23
  33.0 0.3 fusion.28
  33.3 0.4 copy-done.4
  33.7 0.5 fusion.15
  34.2 0.1 copy-done.2
  34.3 1.0 copy-done.11
  35.3 0.5 convolution_convert_fusion.4
  35.8 0.8 copy-done.1
  36.6 2.5 fusion.41
  39.1 2.4 all-reduce.2
  41.6 0.0 copy-start.8
  41.6 0.0 copy-start.10
  41.6 3.4 add_convert_fusion
  45.0 0.0 all-gather.3.cloned.1.call-update
  45.0 0.0 all-gather.5.cloned.1.call-start
  45.0 0.7 all-gather.5.cloned.1.call-update
  45.7 0.0 reduce-scatter.3.cloned.1.call-start
  45.8 8.7 %all-gather.3.cloned.1.call-done = bf16[256,5120]{1,0:T(8,128)(2,1)} async-done(((bf16[256,2560]{1,0:T(8,128)(2,1)}), bf16[256,5120]{1,0:T(8,128)(2,1)}) %all-gather.3.cloned.1.call-update) | async-done | bytes 2621456 | tf_op jit(solution)/shard_map/all_gather | solution.py:113
  54.5 285.4 %all-gather.5.cloned.1.call-done = bf16[5120,2560]{1,0:T(8,128)(2,1)} async-done(((bf16[320,2560]{1,0:T(8,128)(2,1)}), bf16[5120,2560]{1,0:T(8,128)(2,1)}) %all-gather.5.cloned.1.call-update) | async-done | bytes 26214416 | tf_op jit(solution)/shard_map/all_gather | solution.py:96
  339.8 14.3 %multiply_reduce_fusion.1 = (f32[256]{0:T(256)S(1)}, f32[256]{0:T(256)S(1)}, f32[256,2560]{1,0:T(8,128)}) fusion(bf16[256,2560]{1,0:T(8,128)(2,1)} %param.27, f32[2560]{0:T(1024)S(1)} %copy-done.8, f32[2560]{0:T(1024)S(1)} %copy-done.10, bf16[256,5120]{1,0:T(8,128)(2,1)} %all-gather.3.cloned.1.call-done, bf16[5120,2560]{1,0:T(8,128)(2,1)} %all-gather.5.cloned.1.call-done), kind=kOutput, calls=%fused_computation.9 | convolution fusion | flops 6715473920 | bytes 32790528 | tf_op jit(solution)/shard_map/dot_general | solution.py:17
  354.2 2.4 all-reduce.1
  356.6 14.8 %convolution_convert_fusion = bf16[256,5120]{1,0:T(8,128)(2,1)} fusion(bf16[5120,2560]{1,0:T(8,128)(2,1)} %all-gather.5.cloned.1.call-done, f32[256,2560]{1,0:T(8,128)} %get-tuple-element.23, bf16[256,2560]{1,0:T(8,128)(2,1)} %param.27, f32[256]{0:T(256)S(1)} %get-tuple-element.16, f32[256]{0:T(256)S(1)} %broadcast_multiply_fusion.3, f32[2560]{0:T(1024)S(1)} %copy-done.8, ...), kind=kOutput, calls=%fused_computation | convolution fusion | flops 6716784640 | bytes 32781312 | tf_op jit(solution)/shard_map/dot_general | solution.py:21
  371.5 0.0 reduce-scatter.3.cloned.1.call-update
  371.5 0.2 all-reduce.5.cloned.1.call-start
  371.7 8.3 %reduce-scatter.3.cloned.1.call-done = bf16[256,2560]{1,0:T(8,128)(2,1)} async-done(((bf16[256,5120]{1,0:T(8,128)(2,1)}), bf16[256,2560]{1,0:T(8,128)(2,1)}) %reduce-scatter.3.cloned.1.call-update) | async-done | bytes 1310736 | tf_op jit(solution)/shard_map/reduce_scatter | solution.py:124
  380.0 2.9 fusion
  382.9 2.5 all-reduce
  385.4 4.2 multiply_convert_fusion
  389.5 3.8 fusion.5
  393.3 3.2 fusion.7
  396.5 1.9 fusion.40
  398.4 0.0 copy-start.5
  398.4 1.9 reshape.158
  400.3 1.9 multiply_reduce_fusion.4
  402.2 0.1 reshape.159
  402.3 0.6 pad_maximum_fusion
  402.9 0.0 all-reduce.5.cloned.1.call-update
  403.0 0.0 reduce-scatter.5.cloned.1.call-start
  403.0 3.7 convolution_convert_fusion.1
  406.7 0.0 reduce-scatter.5.cloned.1.call-update
  406.7 3.1 multiply_convert_fusion.1
  409.8 112.4 %all-reduce.5.cloned.1.call-done = f32[16896]{0:T(1024)} async-done(((f32[16896]{0:T(1024)}), f32[16896]{0:T(1024)}) %all-reduce.5.cloned.1.call-update) | async-done | bytes 67600 | tf_op jit(solution)/shard_map/psum | solution.py:150
  522.2 0.7 slice.73
  522.9 0.7 reshape.160
  523.6 1.5 slice_bitcast_fusion
  525.0 83.8 %reduce-scatter.5.cloned.1.call-done = bf16[32,2560]{1,0:T(8,128)(2,1)} async-done(((bf16[512,2560]{1,0:T(8,128)(2,1)}), bf16[32,2560]{1,0:T(8,128)(2,1)}) %reduce-scatter.5.cloned.1.call-update) | async-done | bytes 163856 | tf_op jit(solution)/shard_map/reduce_scatter | solution.py:137
  608.8 1.7 convert_element_type.120
  (23 shorter events, 0.1 us)
Async XLA Ops:
  7.2 28.6 %copy-start = (bf16[512,2560]{1,0:T(8,128)(2,1)S(1)}, bf16[512,2560]{1,0:T(8,128)(2,1)}, u32[]{:S(2)}) copy-start(bf16[512,2560]{1,0:T(8,128)(2,1)} %param.21) | copy-start | bytes 7864324
  7.2 17.8 %copy-start.9 = (f32[2560]{0:T(1024)S(1)}, f32[2560]{0:T(1024)}, u32[]{:S(2)}) copy-start(f32[2560]{0:T(1024)} %param.23) | copy-start | bytes 30724
  7.2 17.8 %copy-start.6 = (bf16[128,128]{1,0:T(8,128)(2,1)S(1)}, bf16[128,128]{1,0:T(8,128)(2,1)}, u32[]{:S(2)}) copy-start(bf16[128,128]{1,0:T(8,128)(2,1)} %param.20) | copy-start | bytes 98308
  11.7 21.0 %all-to-all-start = ((bf16[16,32,384]{2,1,0:T(8,128)(2,1)}), bf16[16,32,384]{2,1,0:T(8,128)(2,1)S(1)}, u32[]{:S(2)}, u32[]{:S(2)}) async-start(bf16[16,32,384]{2,1,0:T(8,128)(2,1)} %bitcast.34), calls=%async_computation | async-start | bytes 786432 | tf_op jit(solution)/shard_map/all_to_all | solution.py:65
  20.1 34.4 %all-gather.3.cloned.1.call-start = ((), (), s32[]{:S(2)}) async-start(), calls=%async_computation.3 | async-start | bytes 3932160 | tf_op jit(solution)/shard_map/all_gather | solution.py:113
  32.7 1.0 copy-start.4
  33.3 1.0 copy-start.2
  34.3 1.0 copy-start.11
  35.3 1.3 copy-start.1
  36.6 5.0 copy-start.7
  41.6 298.3 %copy-start.8 = (f32[2560]{0:T(1024)S(1)}, f32[2560]{0:T(1024)}, u32[]{:S(2)}) copy-start(f32[2560]{0:T(1024)} %param.26) | copy-start | bytes 30724
  41.6 298.3 %copy-start.10 = (f32[2560]{0:T(1024)S(1)}, f32[2560]{0:T(1024)}, u32[]{:S(2)}) copy-start(f32[2560]{0:T(1024)} %param.25) | copy-start | bytes 30724
  45.0 294.8 %all-gather.5.cloned.1.call-start = ((), (), s32[]{:S(2)}) async-start(), calls=%async_computation.4 | async-start | bytes 27852800 | tf_op jit(solution)/shard_map/all_gather | solution.py:96
  45.7 334.3 %reduce-scatter.3.cloned.1.call-start = ((), (), s32[]{:S(2)}) async-start(), calls=%async_computation.5 | async-start | bytes 3932160 | tf_op jit(solution)/shard_map/reduce_scatter | solution.py:124
  371.5 150.7 %all-reduce.5.cloned.1.call-start = ((), (), s32[]{:S(2)}) async-start(), calls=%async_computation.7 | async-start | bytes 139264 | tf_op jit(solution)/shard_map/psum | solution.py:150
  396.5 2.0 copy-start.3
  398.4 2.0 copy-start.5
  403.0 205.8 %reduce-scatter.5.cloned.1.call-start = ((), (), s32[]{:S(2)}) async-start(), calls=%async_computation.6 | async-start | bytes 2785280 | tf_op jit(solution)/shard_map/reduce_scatter | solution.py:137
Sparse Core Ops, SparseCore 0:
  45.1 9.3 all-gather.2
  57.1 282.6 all-gather.4
  371.6 8.3 reduce-scatter.2
  403.1 119.0 all-reduce.4
  524.5 84.3 reduce-scatter.4

commit v2 on v1

--- a/solution.py
+++ b/solution.py
@@ -2,7 +2,11 @@
 import jax.numpy as jnp
 import numpy as np
 from jax import lax
+from jax.experimental import pallas as pl
+from jax.experimental.pallas import tpu as pltpu
 from jax.sharding import PartitionSpec as P
+
+MESH = pl.DeviceIdType.MESH
 
 epsilon = 1e-06
 F32, BF16 = jnp.float32, jnp.bfloat16
@@ -71,6 +75,233 @@
     return incoming[:, :width], slot_recv
 
 
+def place_here():
+    me, core = lax.axis_index("seq"), lax.axis_index("tp")
+    return me // 4, (me // 2) % 2, me % 2, core
+
+
+def greet(devices, count):
+    barrier = pltpu.get_barrier_semaphore()
+    for condition, device in devices:
+
+        def say(device=device):
+            pl.semaphore_signal(barrier, inc=1, device_id=device, device_id_type=MESH)
+
+        if condition is None:
+            say()
+        else:
+            pl.when(condition)(say)
+    pl.semaphore_wait(barrier, count)
+
+
+def gather_kernel(w_ref, out_ref, own_sem, up_send, up_recv, down_send, down_recv, send_sem, recv_sem):
+    z, y, x, core = place_here()
+    half = w_ref.shape[0] // 2
+    rows_a, rows_b = pl.ds(0, half), pl.ds(half, half)
+    last = 3
+
+    def device(zz, yy, xx):
+        return (zz * 4 + yy * 2 + xx, core)
+
+    x_side, y_side = device(z, y, 1 - x), device(z, 1 - y, x)
+    above, below = device(jnp.minimum(z + 1, last), y, x), device(jnp.maximum(z - 1, 0), y, x)
+    greet(
+        [(None, x_side), (None, y_side), (z < last, above), (z > 0, below)],
+        2 + (z < last).astype(jnp.int32) + (z > 0).astype(jnp.int32),
+    )
+
+    def remote(src, dst, sems, target):
+        return pltpu.make_async_remote_copy(
+            src_ref=src, dst_ref=dst, send_sem=sems[0], recv_sem=sems[1], device_id=target, device_id_type=MESH
+        )
+
+    def line_copy(zz, step, up, src=None):
+        block = out_ref.at[zz, y, x]
+        send, recv = (up_send, up_recv) if up else (down_send, down_recv)
+        return remote(block if src is None else src, block, (send.at[step], recv.at[step]), above if up else below)
+
+    kinds = (
+        (y, x, rows_a, True),
+        (y, x, rows_b, False),
+        (y, x, rows_a, False),
+        (y, x, rows_b, True),
+        (y, 1 - x, rows_a, False),
+        (1 - y, x, rows_b, True),
+    )
+
+    def plane_copy(kind, zz, own=False):
+        yy, xx, rows, to_x = kinds[kind]
+        block = out_ref.at[zz, yy, xx, rows]
+        return remote(
+            w_ref.at[rows] if own else block,
+            block,
+            (send_sem.at[kind, zz], recv_sem.at[kind, zz]),
+            x_side if to_x else y_side,
+        )
+
+    def arrival(kind, zz):
+        yy, xx, rows, to_x = kinds[kind]
+        yy, xx = (yy, 1 - xx) if to_x else (1 - yy, xx)
+        block = out_ref.at[zz, yy, xx, rows]
+        return remote(block, block, (send_sem.at[kind, zz], recv_sem.at[kind, zz]), x_side if to_x else y_side)
+
+    def relay(zz):
+        arrival(0, zz).wait_recv()
+        plane_copy(4, zz).start()
+        arrival(1, zz).wait_recv()
+        plane_copy(5, zz).start()
+
+    pl.when(z < last)(lambda: line_copy(z, 0, True, w_ref).start())
+    pl.when(z > 0)(lambda: line_copy(z, 0, False, w_ref).start())
+    for kind in range(4):
+        plane_copy(kind, z, True).start()
+    own = pltpu.make_async_copy(w_ref, out_ref.at[z, y, x], own_sem)
+    own.start()
+    for step in range(1, 4):
+        for up in (True, False):
+            zz = z - step if up else z + step
+            came = zz >= 0 if up else zz <= last
+            goes_on = jnp.logical_and(came, z < last if up else z > 0)
+
+            def arrive(zz=zz, step=step, up=up):
+                line_copy(zz, step - 1, up).wait_recv()
+
+            def pass_on(zz=zz, step=step, up=up):
+                line_copy(zz, step, up).start()
+
+            def spread(zz=zz):
+                for kind in range(4):
+                    plane_copy(kind, zz).start()
+
+            pl.when(came)(arrive)
+            if step < 3:
+                pl.when(goes_on)(pass_on)
+            pl.when(came)(spread)
+        if step == 1:
+            relay(z)
+        else:
+            for zz, came in ((z - step + 1, z - step + 1 >= 0), (z + step - 1, z + step - 1 <= last)):
+                pl.when(came)(lambda zz=zz: relay(zz))
+    for zz, came in ((z - 3, z - 3 >= 0), (z + 3, z + 3 <= last)):
+        pl.when(came)(lambda zz=zz: relay(zz))
+    own.wait()
+    for zz in range(4):
+        for kind in range(2, 6):
+            arrival(kind, zz).wait_recv()
+        for kind in range(6):
+            plane_copy(kind, zz).wait_send()
+    for step in range(3):
+        pl.when(jnp.logical_and(z - step >= 0, z < last))(
+            lambda step=step: line_copy(z - step, step, True).wait_send()
+        )
+        pl.when(jnp.logical_and(z + step <= last, z > 0))(
+            lambda step=step: line_copy(z + step, step, False).wait_send()
+        )
+
+
+def gather_weights(w_query):
+    depth, columns = w_query.shape
+    dma = pltpu.SemaphoreType.DMA
+    out = pl.pallas_call(
+        gather_kernel,
+        out_shape=jax.ShapeDtypeStruct((4, 2, 2, depth, columns), w_query.dtype),
+        in_specs=[pl.BlockSpec(memory_space=pl.ANY)],
+        out_specs=pl.BlockSpec(memory_space=pl.ANY),
+        scratch_shapes=[dma, dma((3,)), dma((3,)), dma((3,)), dma((3,)), dma((6, 4)), dma((6, 4))],
+        compiler_params=pltpu.CompilerParams(collective_id=0, has_side_effects=True),
+    )(w_query)
+    return out.reshape(16 * depth, columns)
+
+
+def reduce_kernel(
+    p_ref, g_ref, out_ref, small_ref, one_a, one_b, sum_a, sum_b, two_a, two_b, line, line_in,
+    small, small_in, small_z, send_sem, recv_sem, line_send, line_recv, g_send, g_recv, gz_send, gz_recv,
+):
+    z, y, x, core = place_here()
+    half = p_ref.shape[-1] // 2
+    cols_a, cols_b = pl.ds(0, half), pl.ds(half, half)
+
+    def device(zz, yy, xx, cc):
+        return (zz * 4 + yy * 2 + xx, cc)
+
+    x_side, y_side, core_side = device(z, y, 1 - x, core), device(z, 1 - y, x, core), device(z, y, x, 1 - core)
+    peers = [lax.rem(z + d, 4) for d in (1, 2, 3)]
+    greet([(None, t) for t in [x_side, y_side, core_side] + [device(p, y, x, core) for p in peers]], 6)
+
+    def send(src, dst, sems, target):
+        copy = pltpu.make_async_remote_copy(
+            src_ref=src, dst_ref=dst, send_sem=sems[0], recv_sem=sems[1], device_id=target, device_id_type=MESH
+        )
+        copy.start()
+        return copy
+
+    def sems(i):
+        return (send_sem.at[i], recv_sem.at[i])
+
+    def added(a, b):
+        return (a.astype(F32) + b.astype(F32)).astype(BF16)
+
+    first_a = send(p_ref.at[:, :, 1 - x, :, cols_a], one_a, sems(0), x_side)
+    first_b = send(p_ref.at[:, 1 - y, :, :, cols_b], one_b, sems(1), y_side)
+    small[0] = g_ref[...]
+    for i, target in enumerate((core_side, x_side, y_side)):
+        send(small.at[i], small_in.at[i], (g_send.at[i], g_recv.at[i]), target).wait()
+        small[i + 1] = small[i] + small_in[i]
+    small_z[z] = small[3]
+    g_line = [
+        send(small.at[3], small_z.at[z], (gz_send.at[d], gz_recv.at[d]), device(peers[d], y, x, core))
+        for d in range(3)
+    ]
+    first_a.wait()
+    for zz in range(4):
+        for q in range(2):
+            sum_a[zz, q] = added(p_ref[zz, q, x, :, 0:half], one_a[zz, q])
+    second_a = send(sum_a.at[:, 1 - y], two_a, sems(2), y_side)
+    first_b.wait()
+    for zz in range(4):
+        for q in range(2):
+            sum_b[zz, q] = added(p_ref[zz, y, q, :, half:], one_b[zz, q])
+    second_b = send(sum_b.at[:, 1 - x], two_b, sems(3), x_side)
+    second_a.wait()
+    for zz in range(4):
+        line[zz, :, 0:half] = added(sum_a[zz, y], two_a[zz])
+    second_b.wait()
+    for zz in range(4):
+        line[zz, :, half:] = added(sum_b[zz, x], two_b[zz])
+    last = [
+        send(line.at[peers[d]], line_in.at[d], (line_send.at[d], line_recv.at[d]), device(peers[d], y, x, core))
+        for d in range(3)
+    ]
+    for copy in g_line:
+        copy.wait()
+    small_ref[...] = (small_z[0] + small_z[1]) + (small_z[2] + small_z[3])
+    for copy in last:
+        copy.wait()
+    total = line[z].astype(F32)
+    for d in range(3):
+        total = total + line_in[d].astype(F32)
+    out_ref[...] = total
+
+
+def reduce_grads(partial, small):
+    rows, columns = partial.shape
+    piece, half = rows // 16, columns // 2
+    dma = pltpu.SemaphoreType.DMA
+    vmem = pl.BlockSpec(memory_space=pltpu.VMEM)
+    return pl.pallas_call(
+        reduce_kernel,
+        out_shape=(jax.ShapeDtypeStruct((piece, columns), F32), jax.ShapeDtypeStruct(small.shape, F32)),
+        in_specs=[vmem, vmem],
+        out_specs=(vmem, vmem),
+        scratch_shapes=[pltpu.VMEM((4, 2, piece, half), BF16)] * 4
+        + [pltpu.VMEM((4, piece, half), BF16)] * 2
+        + [pltpu.VMEM((4, piece, columns), BF16), pltpu.VMEM((3, piece, columns), BF16)]
+        + [pltpu.VMEM((4,) + small.shape, F32), pltpu.VMEM((3,) + small.shape, F32), pltpu.VMEM((4,) + small.shape, F32)]
+        + [dma((4,)), dma((4,)), dma((3,)), dma((3,)), dma((3,)), dma((3,)), dma((3,)), dma((3,))],
+        compiler_params=pltpu.CompilerParams(collective_id=1, has_side_effects=True, vmem_limit_bytes=32 << 20),
+    )(partial.reshape(4, 2, 2, piece, columns), small)
+
+
 def body(
     latent,
     pose_rows,
@@ -93,7 +324,11 @@
     query_width = w_query.shape[1] * tp_count
     depth, c_one = w_section1.shape
     c_two = w_section2.shape[1]
-    weights_all = lax.all_gather(w_query, "seq", axis=0, tiled=True)
+    chips = seq_count == 16 and tp_count == 2
+    if chips:
+        weights_all = gather_weights(w_query)
+    else:
+        weights_all = lax.all_gather(w_query, "seq", axis=0, tiled=True)
     pose_in, slot_recv = dispatch(pose_rows, dest_device, dest_slot, seq_count)
     w_wide = spread_one(w_section1)
     w_quad = jnp.kron(jnp.eye(4, dtype=BF16), w_section2)
@@ -134,9 +369,7 @@
         - normed * (grad_cross / full_width)[:, None]
     )
     latent_grad = latent_grad.astype(BF16)
-    section_three_grad = lax.psum_scatter(
-        mm_tn(token_two, latent_grad).astype(BF16), "seq", scatter_dimension=0, tiled=True
-    ).astype(F32)
+    partial_three = mm_tn(token_two, latent_grad).astype(BF16)
     token_grad = mm_nt(latent_grad, w_section3).astype(BF16)
     stacked_grad = mm_tn(select, token_grad)
     two_grad = (stacked_grad * silu_slope(z_two)).astype(BF16)
@@ -147,8 +380,14 @@
     one_grad = (mm_nt(two_grad, w_quad) * silu_slope(z_one)).astype(BF16)
     grad_one = fold_one(mm_tn(pose_in, one_grad), depth, c_one)
     packed = jnp.concatenate([grad_two.reshape(-1), grad_one.reshape(-1)])
-    packed = lax.psum(packed, ("seq", "tp"))
     cut = grad_two.size
+    if chips:
+        padded = jnp.pad(packed, (0, -packed.size % 1024)).reshape(-1, 128)
+        section_three_grad, packed = reduce_grads(partial_three, padded)
+        packed = packed.reshape(-1)[: cut + grad_one.size]
+    else:
+        section_three_grad = lax.psum_scatter(partial_three, "seq", scatter_dimension=0, tiled=True).astype(F32)
+        packed = lax.psum(packed, ("seq", "tp"))
     return (
         normed_query,
         section_three_grad,

time: 618 us -> 382 us (0.62)
  waiting for transfers between devices: 506 us -> 12.4 us
  Pallas kernels: 0 us -> 260 us
    all_gather x1 -> x0, waiting for transfers between devices: 285 us -> none  [body(): weights_all = lax.all_gather(w_query, 'seq', axis=0, tiled=True)]
    pallas_call x0 -> x2, Pallas kernels: none -> 260 us  [the longest x1 216 us: gather_weights(): pl.pallas_call(gather_kernel, out_shape=jax.ShapeDtypeStruct((4, 2, 2, de...]
    psum x1 -> x0, waiting for transfers between devices: 112 us -> none  [body(): packed = lax.psum(packed, ('seq', 'tp'))]
    reduce_scatter x1 -> x0, waiting for transfers between devices: 83.8 us -> none  [body(): lax.psum_scatter(mm_tn(token_two, latent_grad).astype(BF16), 'seq', scatt...]
    all_gather x1, waiting for transfers between devices: 8.67 us -> 0.02 us  [body(): whole = lax.all_gather(modulated, 'tp', axis=1, tiled=True)]
  transfers between devices with their start and end apart: 6 -> 3, of which waited for: 6 -> 2; matrix products, arithmetic and copies ran while one was open for 3% -> 2% of each run, Pallas kernels for 0% -> 57%
where the time goes in v2:
time: 382 us; the launch traced here: 381 us
  Pallas kernels  260 us (68%)
  matrix products  47.1 us (12%)
  other arithmetic  20.9 us (5%)
  between operations  14.3 us (4%)
  waiting for transfers between devices  12.4 us (3%)
  local copies, waits for them, and re-layouts  10.2 us (3%)
  starting transfers between devices  8.4 us (2%)
  blocking collectives  7.54 us (2%)
    pallas_call x1, Pallas kernels, gather_weights(): pl.pallas_call(gather_kernel, out_shape=jax.ShapeDtypeStruct((4, 2, 2, de...  216 us
    pallas_call x1, Pallas kernels, reduce_grads(): pl.pallas_call(reduce_kernel, out_shape=(jax.ShapeDtypeStruct((piece, col...  43.9 us
    dot_general x7, matrix products, mm(): return jnp.dot(a, b, preferred_element_type=F32)  20.9 us
    dot_general x1, matrix products, mm_nt(): lax.dot_general(a, b, (((1,), (1,)), ((), ())), preferred_element_type=F32)  14.8 us
    dot_general x4, matrix products, mm_tn(): lax.dot_general(a, b, (((0,), (0,)), ((), ())), preferred_element_type=F32)  11.3 us
    all_to_all x1, starting transfers between devices, dispatch(): lax.all_to_all(outgoing.reshape(seq_count, capacity, width + 128), 'seq',...  8.32 us
  transfers between devices with their start and end apart: 3, of which 2 were waited for; matrix products, arithmetic and copies ran while one was open for 2% of the time, Pallas kernels for 57%

profile of v2, /device:TPU:0, one launch (start us, length us, event | category | flops | bytes accessed | tf_op | source)
XLA Modules:
  0.0 380.7 jit_solution(13624963529362301321)
XLA Ops:
  7.2 0.0 copy-start
  7.2 0.0 copy-start.11
  7.2 0.0 copy-start.8
  7.2 1.0 fusion.8
  8.3 0.7 convert_add_fusion
  9.0 0.7 and_select_fusion.1
  9.6 0.1 select_convert_fusion
  9.8 2.0 convolution_convert_fusion.2
  11.7 8.3 %all-to-all-start = ((bf16[16,32,384]{2,1,0:T(8,128)(2,1)}), bf16[16,32,384]{2,1,0:T(8,128)(2,1)S(1)}, u32[]{:S(2)}, u32[]{:S(2)}) async-start(bf16[16,32,384]{2,1,0:T(8,128)(2,1)} %bitcast.39), calls=%async_computation | async-start | bytes 786432 | tf_op jit(solution)/shard_map/all_to_all | solution.py:69
  20.1 0.0 all-gather.2.cloned.1.call-start
  20.1 0.7 convert_element_type.104
  20.8 1.9 multiply_convert_fusion.2
  22.7 2.2 convert_element_type.106
  24.9 0.0 copy-done.11
  25.0 0.0 copy-done.8
  25.0 1.1 broadcast_multiply_fusion
  26.0 6.7 %all-to-all-done = bf16[16,32,384]{2,1,0:T(8,128)(2,1)S(1)} async-done(((bf16[16,32,384]{2,1,0:T(8,128)(2,1)}), bf16[16,32,384]{2,1,0:T(8,128)(2,1)S(1)}, u32[]{:S(2)}, u32[]{:S(2)}) %all-to-all-start) | async-done | bytes 393248 | tf_op jit(solution)/shard_map/all_to_all | solution.py:69
  32.7 0.3 fusion.23
  33.0 0.3 fusion.28
  33.3 0.0 copy-start.4
  33.3 0.4 copy-done.6
  33.7 0.5 fusion.15
  34.2 0.1 copy-done.4
  34.3 1.0 copy-done.13
  35.3 0.5 convolution_convert_fusion.4
  35.8 0.0 copy-done
  35.8 0.8 copy-done.3
  36.6 2.4 fusion.42
  39.0 2.4 all-reduce.3
  41.5 0.0 copy-done.9
  41.5 3.4 add_convert_fusion
  44.8 0.0 all-gather.2.cloned.1.call-update
  44.9 0.0 copy-start.10
  44.9 0.0 copy-start.12
  44.9 0.0 reduce-scatter.2.cloned.1.call-start
  44.9 216.0 %shard_map.174 = bf16[4,2,2,320,2560]{4,3,2,1,0:T(8,128)(2,1)} custom-call(bf16[320,2560]{1,0:T(8,128)(2,1)} %w_ref.1), custom_call_target="tpu_custom_call" | custom-call | tf_op jit(solution)/shard_map/pallas_call | solution.py:205
  260.9 0.0 all-gather.2.cloned.1.call-done
  260.9 0.0 copy-done.10
  261.0 0.0 copy-done.12
  261.0 14.2 %multiply_reduce_fusion.1 = (f32[256]{0:T(256)S(1)}, f32[256]{0:T(256)S(1)}, f32[256,2560]{1,0:T(8,128)}) fusion(bf16[256,2560]{1,0:T(8,128)(2,1)} %param.27, f32[2560]{0:T(1024)S(1)} %copy-done.10, f32[2560]{0:T(1024)S(1)} %copy-done.12, bf16[256,5120]{1,0:T(8,128)(2,1)} %all-gather.2.cloned.1.call-done, bf16[5120,2560]{1,0:T(8,128)(2,1)} %bitcast.32), kind=kOutput, calls=%fused_computation.9 | convolution fusion | flops 6715473920 | bytes 32790528 | tf_op jit(solution)/shard_map/dot_general | solution.py:21
  275.2 2.6 all-reduce.2
  277.8 14.8 %convolution_convert_fusion = bf16[256,5120]{1,0:T(8,128)(2,1)} fusion(bf16[5120,2560]{1,0:T(8,128)(2,1)} %bitcast.33, f32[256,2560]{1,0:T(8,128)} %get-tuple-element.27, bf16[256,2560]{1,0:T(8,128)(2,1)} %param.27, f32[256]{0:T(256)S(1)} %get-tuple-element.20, f32[256]{0:T(256)S(1)} %broadcast_multiply_fusion.3, f32[2560]{0:T(1024)S(1)} %copy-done.10, ...), kind=kOutput, calls=%fused_computation | convolution fusion | flops 6716784640 | bytes 32781312 | tf_op jit(solution)/shard_map/dot_general | solution.py:25
  292.7 0.0 reduce-scatter.2.cloned.1.call-update
  292.7 3.1 multiply_convert_fusion.1
  295.8 5.6 %reduce-scatter.2.cloned.1.call-done = bf16[256,2560]{1,0:T(8,128)(2,1)} async-done(((bf16[256,5120]{1,0:T(8,128)(2,1)}), bf16[256,2560]{1,0:T(8,128)(2,1)}) %reduce-scatter.2.cloned.1.call-update) | async-done | bytes 1310736 | tf_op jit(solution)/shard_map/reduce_scatter | solution.py:359
  301.4 2.9 fusion
  304.3 2.5 all-reduce.1
  306.8 4.2 %multiply_convert_fusion = bf16[256,2560]{1,0:T(8,128)(2,1)} fusion(bf16[256,2560]{1,0:T(8,128)(2,1)} %reduce-scatter.2.cloned.1.call-done, f32[256,2560]{1,0:T(8,128)} %get-tuple-element.26, f32[256]{0:T(256)S(1)} %broadcast_multiply_fusion.1, f32[256]{0:T(256)S(1)} %broadcast_multiply_fusion.2, f32[2560]{0:T(1024)S(1)} %broadcast_add_fusion, ...), kind=kLoop, calls=%fused_computation.4 | loop fusion | flops 5898240 | bytes 5257216 | tf_op jit(solution)/shard_map/convert_element_type | solution.py:371
  310.9 3.8 fusion.5
  314.7 3.2 fusion.7
  317.9 2.0 fusion.41
  319.9 0.0 copy-done.2
  319.9 0.0 copy-start.5
  319.9 2.4 convolution_convert_fusion.1
  322.3 0.0 copy-done.5
  322.3 1.9 reshape.159
  324.2 0.0 copy-done.7
  324.2 1.9 multiply_reduce_fusion.4
  326.1 0.1 reshape.160
  326.2 1.7 copy-done.1
  327.9 43.9 %shard_map.175 = (f32[32,2560]{1,0:T(8,128)S(1)}, f32[136,128]{1,0:T(8,128)S(1)}) custom-call(bf16[4,2,2,32,2560]{4,3,2,1,0:T(8,128)(2,1)S(1)} %bitcast.31, f32[136,128]{1,0:T(8,128)S(1)} %fusion.33.g_ref), custom_call_target="tpu_custom_call" | custom-call | tf_op jit(solution)/shard_map/pallas_call | solution.py:291
  371.9 0.6 slice.48
  372.5 0.7 reshape.162
  373.2 0.7 copy.31
  (20 shorter events, 0.1 us)
Async XLA Ops:
  7.2 28.6 %copy-start = (bf16[512,2560]{1,0:T(8,128)(2,1)S(1)}, bf16[512,2560]{1,0:T(8,128)(2,1)}, u32[]{:S(2)}) copy-start(bf16[512,2560]{1,0:T(8,128)(2,1)} %param.21) | copy-start | bytes 7864324
  7.2 17.8 %copy-start.11 = (f32[2560]{0:T(1024)S(1)}, f32[2560]{0:T(1024)}, u32[]{:S(2)}) copy-start(f32[2560]{0:T(1024)} %param.23) | copy-start | bytes 30724
  7.2 17.8 %copy-start.8 = (bf16[128,128]{1,0:T(8,128)(2,1)S(1)}, bf16[128,128]{1,0:T(8,128)(2,1)}, u32[]{:S(2)}) copy-start(bf16[128,128]{1,0:T(8,128)(2,1)} %param.20) | copy-start | bytes 98308
  11.7 21.0 %all-to-all-start = ((bf16[16,32,384]{2,1,0:T(8,128)(2,1)}), bf16[16,32,384]{2,1,0:T(8,128)(2,1)S(1)}, u32[]{:S(2)}, u32[]{:S(2)}) async-start(bf16[16,32,384]{2,1,0:T(8,128)(2,1)} %bitcast.39), calls=%async_computation | async-start | bytes 786432 | tf_op jit(solution)/shard_map/all_to_all | solution.py:69
  20.1 240.9 %all-gather.2.cloned.1.call-start = ((), (), s32[]{:S(2)}) async-start(), calls=%async_computation.2 | async-start | bytes 3932160 | tf_op jit(solution)/shard_map/all_gather | solution.py:348
  32.7 1.0 copy-start.6
  33.3 1.0 copy-start.4
  34.3 1.0 copy-start.13
  35.3 1.3 copy-start.3
  36.6 4.9 %copy-start.9 = (f32[2560]{0:T(1024)S(1)}, f32[2560]{0:T(1024)}, u32[]{:S(2)}) copy-start(f32[2560]{0:T(1024)} %param.22) | copy-start | bytes 30724
  44.9 216.1 %copy-start.10 = (f32[2560]{0:T(1024)S(1)}, f32[2560]{0:T(1024)}, u32[]{:S(2)}) copy-start(f32[2560]{0:T(1024)} %param.26) | copy-start | bytes 30724
  44.9 216.1 %copy-start.12 = (f32[2560]{0:T(1024)S(1)}, f32[2560]{0:T(1024)}, u32[]{:S(2)}) copy-start(f32[2560]{0:T(1024)} %param.25) | copy-start | bytes 30724
  44.9 256.5 %reduce-scatter.2.cloned.1.call-start = ((), (), s32[]{:S(2)}) async-start(), calls=%async_computation.3 | async-start | bytes 3932160 | tf_op jit(solution)/shard_map/reduce_scatter | solution.py:359
  317.9 2.0 copy-start.2
  319.9 2.4 copy-start.5
  322.3 1.9 copy-start.7
  326.2 1.7 copy-start.1
Sparse Core Ops, SparseCore 0:
  45.0 9.3 all-gather.1
  292.8 8.5 reduce-scatter.1

commit v3 on v2

--- a/solution.py
+++ b/solution.py
@@ -94,10 +94,12 @@
     pl.semaphore_wait(barrier, count)
 
 
-def gather_kernel(w_ref, out_ref, own_sem, up_send, up_recv, down_send, down_recv, send_sem, recv_sem):
+def gather_kernel(w_ref, out_ref, own_sem, up_send, up_recv, down_send, down_recv, send_sem, recv_sem, cu_send, cu_recv, cd_send, cd_recv):
     z, y, x, core = place_here()
-    half = w_ref.shape[0] // 2
-    rows_a, rows_b = pl.ds(0, half), pl.ds(half, half)
+    third = w_ref.shape[0] // 80 * 16
+    half = (w_ref.shape[0] - third) // 2
+    rows_a, rows_b, rows_c = pl.ds(0, half), pl.ds(half, half), pl.ds(2 * half, third)
+    rows_c1, rows_c2 = pl.ds(2 * half, third // 2), pl.ds(2 * half + third // 2, third // 2)
     last = 3
 
     def device(zz, yy, xx):
@@ -127,7 +129,22 @@
         (y, x, rows_b, True),
         (y, 1 - x, rows_a, False),
         (1 - y, x, rows_b, True),
-    )
+        (y, x, rows_c, True),
+        (y, x, rows_c, False),
+        (y, 1 - x, rows_c1, False),
+        (1 - y, x, rows_c2, True),
+    )
+    others = ((y, 1 - x), (1 - y, x), (1 - y, 1 - x))
+
+    def thin_copy(spot, zz, step, up):
+        block = out_ref.at[zz, others[spot][0], others[spot][1], rows_c]
+        send, recv = (cu_send, cu_recv) if up else (cd_send, cd_recv)
+        index = spot * 3 + step
+        return remote(block, block, (send.at[index], recv.at[index]), above if up else below)
+
+    def thin_start(spot):
+        pl.when(z < last)(lambda: thin_copy(spot, z, 0, True).start())
+        pl.when(z > 0)(lambda: thin_copy(spot, z, 0, False).start())
 
     def plane_copy(kind, zz, own=False):
         yy, xx, rows, to_x = kinds[kind]
@@ -153,10 +170,17 @@
 
     pl.when(z < last)(lambda: line_copy(z, 0, True, w_ref).start())
     pl.when(z > 0)(lambda: line_copy(z, 0, False, w_ref).start())
-    for kind in range(4):
+    for kind in (6, 7, 0, 1, 2, 3):
         plane_copy(kind, z, True).start()
     own = pltpu.make_async_copy(w_ref, out_ref.at[z, y, x], own_sem)
     own.start()
+    for spot in range(2):
+        arrival(6 + spot, z).wait_recv()
+        plane_copy(8 + spot, z).start()
+        thin_start(spot)
+    arrival(8, z).wait_recv()
+    arrival(9, z).wait_recv()
+    thin_start(2)
     for step in range(1, 4):
         for up in (True, False):
             zz = z - step if up else z + step
@@ -182,6 +206,20 @@
         else:
             for zz, came in ((z - step + 1, z - step + 1 >= 0), (z + step - 1, z + step - 1 <= last)):
                 pl.when(came)(lambda zz=zz: relay(zz))
+        for spot in range(3):
+            for up in (True, False):
+                zz = z - step if up else z + step
+                came = zz >= 0 if up else zz <= last
+
+                def thin_arrive(spot=spot, zz=zz, step=step, up=up):
+                    thin_copy(spot, zz, step - 1, up).wait_recv()
+
+                def thin_on(spot=spot, zz=zz, step=step, up=up):
+                    thin_copy(spot, zz, step, up).start()
+
+                pl.when(came)(thin_arrive)
+                if step < 3:
+                    pl.when(jnp.logical_and(came, z < last if up else z > 0))(thin_on)
     for zz, came in ((z - 3, z - 3 >= 0), (z + 3, z + 3 <= last)):
         pl.when(came)(lambda zz=zz: relay(zz))
     own.wait()
@@ -190,7 +228,16 @@
             arrival(kind, zz).wait_recv()
         for kind in range(6):
             plane_copy(kind, zz).wait_send()
+    for kind in range(6, 10):
+        plane_copy(kind, z).wait_send()
     for step in range(3):
+        for spot in range(3):
+            pl.when(jnp.logical_and(z - step >= 0, z < last))(
+                lambda step=step, spot=spot: thin_copy(spot, z - step, step, True).wait_send()
+            )
+            pl.when(jnp.logical_and(z + step <= last, z > 0))(
+                lambda step=step, spot=spot: thin_copy(spot, z + step, step, False).wait_send()
+            )
         pl.when(jnp.logical_and(z - step >= 0, z < last))(
             lambda step=step: line_copy(z - step, step, True).wait_send()
         )
@@ -207,7 +254,7 @@
         out_shape=jax.ShapeDtypeStruct((4, 2, 2, depth, columns), w_query.dtype),
         in_specs=[pl.BlockSpec(memory_space=pl.ANY)],
         out_specs=pl.BlockSpec(memory_space=pl.ANY),
-        scratch_shapes=[dma, dma((3,)), dma((3,)), dma((3,)), dma((3,)), dma((6, 4)), dma((6, 4))],
+        scratch_shapes=[dma, dma((3,)), dma((3,)), dma((3,)), dma((3,)), dma((10, 4)), dma((10, 4))] + [dma((9,))] * 4,
         compiler_params=pltpu.CompilerParams(collective_id=0, has_side_effects=True),
     )(w_query)
     return out.reshape(16 * depth, columns)

time: 382 us -> 375 us (0.982)
  Pallas kernels: 260 us -> 254 us
    pallas_call x1, Pallas kernels: 216 us -> 210 us  [gather_weights(): pl.pallas_call(gather_kernel, out_shape=jax.ShapeDtypeStruct((4, 2, 2, de...]
  transfers between devices with their start and end apart: 3 -> 3, of which waited for: 2 -> 2; matrix products, arithmetic and copies ran while one was open for 2% -> 2% of each run, Pallas kernels for 57% -> 56%
where the time goes in v3:
time: 375 us; the launch traced here: 374 us
  Pallas kernels  254 us (68%)
  matrix products  47.1 us (13%)
  other arithmetic  20.9 us (6%)
  between operations  14.3 us (4%)
  waiting for transfers between devices  12.4 us (3%)
  local copies, waits for them, and re-layouts  10.2 us (3%)
  starting transfers between devices  8.4 us (2%)
  blocking collectives  7.54 us (2%)
    pallas_call x1, Pallas kernels, gather_weights(): pl.pallas_call(gather_kernel, out_shape=jax.ShapeDtypeStruct((4, 2, 2, de...  210 us
    pallas_call x1, Pallas kernels, reduce_grads(): pl.pallas_call(reduce_kernel, out_shape=(jax.ShapeDtypeStruct((piece, col...  44 us
    dot_general x7, matrix products, mm(): return jnp.dot(a, b, preferred_element_type=F32)  20.9 us
    dot_general x1, matrix products, mm_nt(): lax.dot_general(a, b, (((1,), (1,)), ((), ())), preferred_element_type=F32)  14.8 us
    dot_general x4, matrix products, mm_tn(): lax.dot_general(a, b, (((0,), (0,)), ((), ())), preferred_element_type=F32)  11.3 us
    all_to_all x1, starting transfers between devices, dispatch(): lax.all_to_all(outgoing.reshape(seq_count, capacity, width + 128), 'seq',...  8.32 us
  transfers between devices with their start and end apart: 3, of which 2 were waited for; matrix products, arithmetic and copies ran while one was open for 2% of the time, Pallas kernels for 56%

profile of v3, /device:TPU:0, one launch (start us, length us, event | category | flops | bytes accessed | tf_op | source)
XLA Modules:
  0.0 374.3 jit_solution(1555263557180618860)
XLA Ops:
  7.2 0.0 copy-start
  7.2 0.0 copy-start.11
  7.2 0.0 copy-start.8
  7.2 1.0 fusion.8
  8.3 0.7 convert_add_fusion
  9.0 0.7 and_select_fusion.1
  9.6 0.1 select_convert_fusion
  9.8 2.0 convolution_convert_fusion.2
  11.7 8.3 %all-to-all-start = ((bf16[16,32,384]{2,1,0:T(8,128)(2,1)}), bf16[16,32,384]{2,1,0:T(8,128)(2,1)S(1)}, u32[]{:S(2)}, u32[]{:S(2)}) async-start(bf16[16,32,384]{2,1,0:T(8,128)(2,1)} %bitcast.39), calls=%async_computation | async-start | bytes 786432 | tf_op jit(solution)/shard_map/all_to_all | solution.py:69
  20.1 0.0 all-gather.2.cloned.1.call-start
  20.1 0.7 convert_element_type.104
  20.8 1.9 multiply_convert_fusion.2
  22.7 2.2 convert_element_type.106
  24.9 0.0 copy-done.11
  25.0 0.0 copy-done.8
  25.0 1.1 broadcast_multiply_fusion
  26.0 6.7 %all-to-all-done = bf16[16,32,384]{2,1,0:T(8,128)(2,1)S(1)} async-done(((bf16[16,32,384]{2,1,0:T(8,128)(2,1)}), bf16[16,32,384]{2,1,0:T(8,128)(2,1)S(1)}, u32[]{:S(2)}, u32[]{:S(2)}) %all-to-all-start) | async-done | bytes 393248 | tf_op jit(solution)/shard_map/all_to_all | solution.py:69
  32.7 0.3 fusion.23
  33.0 0.3 fusion.28
  33.3 0.0 copy-start.4
  33.3 0.4 copy-done.6
  33.7 0.5 fusion.15
  34.2 0.1 copy-done.4
  34.3 1.0 copy-done.13
  35.3 0.5 convolution_convert_fusion.4
  35.8 0.0 copy-done
  35.8 0.8 copy-done.3
  36.6 2.4 fusion.42
  39.0 2.4 all-reduce.3
  41.5 0.0 copy-done.9
  41.5 3.4 add_convert_fusion
  44.8 0.0 all-gather.2.cloned.1.call-update
  44.9 0.0 copy-start.10
  44.9 0.0 copy-start.12
  44.9 0.0 reduce-scatter.2.cloned.1.call-start
  44.9 209.6 %shard_map.174 = bf16[4,2,2,320,2560]{4,3,2,1,0:T(8,128)(2,1)} custom-call(bf16[320,2560]{1,0:T(8,128)(2,1)} %w_ref.1), custom_call_target="tpu_custom_call" | custom-call | tf_op jit(solution)/shard_map/pallas_call | solution.py:252
  254.5 0.0 all-gather.2.cloned.1.call-done
  254.6 0.0 copy-done.10
  254.6 0.0 copy-done.12
  254.6 14.2 %multiply_reduce_fusion.1 = (f32[256]{0:T(256)S(1)}, f32[256]{0:T(256)S(1)}, f32[256,2560]{1,0:T(8,128)}) fusion(bf16[256,2560]{1,0:T(8,128)(2,1)} %param.27, f32[2560]{0:T(1024)S(1)} %copy-done.10, f32[2560]{0:T(1024)S(1)} %copy-done.12, bf16[256,5120]{1,0:T(8,128)(2,1)} %all-gather.2.cloned.1.call-done, bf16[5120,2560]{1,0:T(8,128)(2,1)} %bitcast.32), kind=kOutput, calls=%fused_computation.9 | convolution fusion | flops 6715473920 | bytes 32790528 | tf_op jit(solution)/shard_map/dot_general | solution.py:21
  268.8 2.6 all-reduce.2
  271.4 14.8 %convolution_convert_fusion = bf16[256,5120]{1,0:T(8,128)(2,1)} fusion(bf16[5120,2560]{1,0:T(8,128)(2,1)} %bitcast.33, f32[256,2560]{1,0:T(8,128)} %get-tuple-element.27, bf16[256,2560]{1,0:T(8,128)(2,1)} %param.27, f32[256]{0:T(256)S(1)} %get-tuple-element.20, f32[256]{0:T(256)S(1)} %broadcast_multiply_fusion.3, f32[2560]{0:T(1024)S(1)} %copy-done.10, ...), kind=kOutput, calls=%fused_computation | convolution fusion | flops 6716784640 | bytes 32781312 | tf_op jit(solution)/shard_map/dot_general | solution.py:25
  286.3 0.0 reduce-scatter.2.cloned.1.call-update
  286.3 3.1 multiply_convert_fusion.1
  289.4 5.6 %reduce-scatter.2.cloned.1.call-done = bf16[256,2560]{1,0:T(8,128)(2,1)} async-done(((bf16[256,5120]{1,0:T(8,128)(2,1)}), bf16[256,2560]{1,0:T(8,128)(2,1)}) %reduce-scatter.2.cloned.1.call-update) | async-done | bytes 1310736 | tf_op jit(solution)/shard_map/reduce_scatter | solution.py:406
  295.0 2.9 fusion
  297.9 2.5 all-reduce.1
  300.4 4.2 %multiply_convert_fusion = bf16[256,2560]{1,0:T(8,128)(2,1)} fusion(bf16[256,2560]{1,0:T(8,128)(2,1)} %reduce-scatter.2.cloned.1.call-done, f32[256,2560]{1,0:T(8,128)} %get-tuple-element.26, f32[256]{0:T(256)S(1)} %broadcast_multiply_fusion.1, f32[256]{0:T(256)S(1)} %broadcast_multiply_fusion.2, f32[2560]{0:T(1024)S(1)} %broadcast_add_fusion, ...), kind=kLoop, calls=%fused_computation.4 | loop fusion | flops 5898240 | bytes 5257216 | tf_op jit(solution)/shard_map/convert_element_type | solution.py:418
  304.5 3.8 %fusion.5 = bf16[512,512]{1,0:T(8,128)(2,1)} fusion(bf16[256,2560]{1,0:T(8,128)(2,1)} %multiply_convert_fusion, bf16[512,2560]{1,0:T(8,128)(2,1)S(1)} %copy-done, f32[512,512]{1,0:T(8,128)} %copy-done.13, s32[512]{0:T(512)S(1)} %fusion.23), kind=kOutput, calls=%fused_computation.24 | convolution fusion | flops 807927808 | bytes 5507072 | tf_op jit(solution)/shard_map/dot_general | solution.py:29
  308.3 3.2 fusion.7
  311.5 2.0 fusion.41
  313.5 0.0 copy-done.2
  313.5 0.0 copy-start.5
  313.5 2.4 convolution_convert_fusion.1
  315.9 0.0 copy-done.5
  315.9 1.9 reshape.159
  317.8 0.0 copy-done.7
  317.8 1.9 multiply_reduce_fusion.4
  319.7 0.1 reshape.160
  319.8 1.7 copy-done.1
  321.5 44.0 %shard_map.175 = (f32[32,2560]{1,0:T(8,128)S(1)}, f32[136,128]{1,0:T(8,128)S(1)}) custom-call(bf16[4,2,2,32,2560]{4,3,2,1,0:T(8,128)(2,1)S(1)} %bitcast.31, f32[136,128]{1,0:T(8,128)S(1)} %fusion.33.g_ref), custom_call_target="tpu_custom_call" | custom-call | tf_op jit(solution)/shard_map/pallas_call | solution.py:338
  365.5 0.6 slice.48
  366.1 0.7 reshape.162
  366.8 0.7 copy.31
  (20 shorter events, 0.1 us)
Async XLA Ops:
  7.2 28.6 %copy-start = (bf16[512,2560]{1,0:T(8,128)(2,1)S(1)}, bf16[512,2560]{1,0:T(8,128)(2,1)}, u32[]{:S(2)}) copy-start(bf16[512,2560]{1,0:T(8,128)(2,1)} %param.21) | copy-start | bytes 7864324
  7.2 17.8 %copy-start.11 = (f32[2560]{0:T(1024)S(1)}, f32[2560]{0:T(1024)}, u32[]{:S(2)}) copy-start(f32[2560]{0:T(1024)} %param.23) | copy-start | bytes 30724
  7.2 17.8 %copy-start.8 = (bf16[128,128]{1,0:T(8,128)(2,1)S(1)}, bf16[128,128]{1,0:T(8,128)(2,1)}, u32[]{:S(2)}) copy-start(bf16[128,128]{1,0:T(8,128)(2,1)} %param.20) | copy-start | bytes 98308
  11.7 21.0 %all-to-all-start = ((bf16[16,32,384]{2,1,0:T(8,128)(2,1)}), bf16[16,32,384]{2,1,0:T(8,128)(2,1)S(1)}, u32[]{:S(2)}, u32[]{:S(2)}) async-start(bf16[16,32,384]{2,1,0:T(8,128)(2,1)} %bitcast.39), calls=%async_computation | async-start | bytes 786432 | tf_op jit(solution)/shard_map/all_to_all | solution.py:69
  20.1 234.5 %all-gather.2.cloned.1.call-start = ((), (), s32[]{:S(2)}) async-start(), calls=%async_computation.2 | async-start | bytes 3932160 | tf_op jit(solution)/shard_map/all_gather | solution.py:395
  32.7 1.0 copy-start.6
  33.3 1.0 copy-start.4
  34.3 1.0 copy-start.13
  35.3 1.3 copy-start.3
  36.6 4.9 %copy-start.9 = (f32[2560]{0:T(1024)S(1)}, f32[2560]{0:T(1024)}, u32[]{:S(2)}) copy-start(f32[2560]{0:T(1024)} %param.22) | copy-start | bytes 30724
  44.9 209.7 %copy-start.10 = (f32[2560]{0:T(1024)S(1)}, f32[2560]{0:T(1024)}, u32[]{:S(2)}) copy-start(f32[2560]{0:T(1024)} %param.26) | copy-start | bytes 30724
  44.9 209.7 %copy-start.12 = (f32[2560]{0:T(1024)S(1)}, f32[2560]{0:T(1024)}, u32[]{:S(2)}) copy-start(f32[2560]{0:T(1024)} %param.25) | copy-start | bytes 30724
  44.9 250.2 %reduce-scatter.2.cloned.1.call-start = ((), (), s32[]{:S(2)}) async-start(), calls=%async_computation.3 | async-start | bytes 3932160 | tf_op jit(solution)/shard_map/reduce_scatter | solution.py:406
  311.5 2.0 copy-start.2
  313.5 2.4 copy-start.5
  315.9 1.9 copy-start.7
  319.7 1.7 copy-start.1
Sparse Core Ops, SparseCore 0:
  45.0 9.3 all-gather.1
  286.4 8.5 reduce-scatter.1
